TPU v7x, 32 devices: a whole 2x2x4 slice. The times are simulated.
32 devices in a mesh: rows: 16 (over z, y, x), cols: 2 (over core).
Axes of the slice: x: 2, y: 2, z: 4, core: 2. Of those that a mesh axis runs over, the one named last changes fastest.
Arguments:
- canvas: bfloat16 [128, 256, 256], P('rows', 'cols'), may hold values from -16 to 16
- conv_weight: bfloat16 [3, 3, 256, 512], replicated, may hold values from -0.125 to 0.125
- conv_bias: bfloat16 [512], replicated, may hold values from -3 to 3
- target_gram: float32 [512, 512], P(('rows', 'cols')), may hold values from -6 to 6
Outputs:
- gram: float32 [512, 512], P(('rows', 'cols'))
- grad_canvas: bfloat16 [128, 256, 256], P('rows', 'cols')
All inputs are finite; a program needn't handle non-finite values.
Results may differ from a plain program's by a relative error of at most 0.009.
Values may be sent and summed in bfloat16 or wider, within the bound.
No kernel may reach another device: no remote copies, remote signals or barrier semaphores. Data moves between devices by JAX's collectives and lax.ppermute only.
A program may use at most 64 MiB of HBM per device.

v0:
```python
import functools
import math

import jax
import jax.numpy as jnp
from jax import lax
from jax.experimental import pallas as pl
from jax.experimental.pallas import tpu as pltpu
from jax.sharding import PartitionSpec as P

gelu_scale = math.sqrt(2.0 / math.pi)
tile = 128
edge = 16
f32, bf16 = jnp.float32, jnp.bfloat16


def tile_pairs(width):
    count = width // tile
    return [(i, j) for i in range(count) for j in range(i, count)]


def shift_rows(last, first):
    count = lax.axis_size("rows")
    forward = [(i, i + 1) for i in range(count - 1)]
    backward = [(target, source) for source, target in forward]
    return lax.ppermute(last, "rows", forward), lax.ppermute(first, "rows", backward)


def shift_cols(last, first):
    count = lax.axis_size("cols")
    forward = [(i, i + 1) for i in range(count - 1)]
    backward = [(target, source) for source, target in forward]
    return lax.ppermute(last, "cols", forward), lax.ppermute(first, "cols", backward)


def device_index():
    return lax.axis_index("rows") * lax.axis_size("cols") + lax.axis_index("cols")


def swap(value, bit):
    total = lax.axis_size("rows") * lax.axis_size("cols")
    return lax.ppermute(value, ("rows", "cols"), [(i, i ^ (1 << bit)) for i in range(total)])


def local(body, out_shape, name, *operands, **kwargs):
    return pl.pallas_call(
        body,
        out_shape=out_shape,
        in_specs=[pl.BlockSpec(memory_space=pltpu.VMEM)] * len(operands),
        compiler_params=pltpu.CompilerParams(vmem_limit_bytes=8 * 1024 * 1024),
        name=name,
        **kwargs,
    )(*operands)


def side_of(bit):
    return lax.rem(device_index() // (1 << bit), 2)


def rows_at(index, count):
    return pl.ds(pl.multiple_of(index * count, count), count)


def halve(keep, got, bit):
    half = keep.shape[0] // 2

    def body(keep_ref, got_ref, send_ref, stay_ref):
        side = side_of(bit)
        away, here = rows_at(1 - side, half), rows_at(side, half)
        send_ref[...] = (keep_ref[away, :] + got_ref[away, :].astype(f32)).astype(bf16)
        stay_ref[...] = keep_ref[here, :] + got_ref[here, :].astype(f32)

    shape = (half, keep.shape[1])
    return local(
        body,
        (jax.ShapeDtypeStruct(shape, bf16), jax.ShapeDtypeStruct(shape, f32)),
        "halve",
        keep,
        got,
    )


def add(keep, got):
    def body(keep_ref, got_ref, sum_ref):
        sum_ref[...] = (keep_ref[...].astype(f32) + got_ref[...].astype(f32)).astype(bf16)

    return local(body, jax.ShapeDtypeStruct(got.shape, bf16), "add", keep, got)


def join(mine, other, bit):
    def body(mine_ref, other_ref, both_ref):
        side = side_of(bit)
        both_ref[:, pl.ds(side, 1)] = mine_ref[...][:, None]
        both_ref[:, pl.ds(1 - side, 1)] = other_ref[...][:, None]

    shape = (mine.shape[0], 2, *mine.shape[1:])
    return local(body, jax.ShapeDtypeStruct(shape, mine.dtype), "join", mine, other)


class Gather:
    def __init__(self, rows):
        self.rows, self.done = rows, []

    def step(self, bit, after):
        share = self.rows.shape[-2:]
        send, _ = lax.optimization_barrier((self.rows, after))
        got = swap(send, bit)
        lead = 1 << sum(other > bit for other in self.done)
        parts = [part.reshape(lead, -1, *share) for part in (send, got)]
        self.rows = join(*parts, bit).reshape(-1, *share)
        self.done.append(bit)


def sum_all(send, keep, gather, order):
    bits = (lax.axis_size("rows") * lax.axis_size("cols")).bit_length() - 1
    halving = list(range(min(3, bits)))
    order = list(order)

    def step(value, bit):
        beside = order.pop(0) if order else None
        got = swap(value, bit)
        if beside is not None:
            gather.step(beside, value)
        return got

    got = step(send, 0)
    for bit in halving[1:]:
        send, keep = halve(keep, got, bit)
        got = step(send, bit)
    mine = add(keep, got)
    for bit in range(len(halving), bits):
        mine = add(mine, step(mine, bit))
    for bit in reversed(halving[1:]):
        got = step(mine, bit)
        mine = join(mine[None], got[None], bit).reshape(-1, mine.shape[1])
    return mine, step(mine, 0), order


def gelu_pair(value):
    square = value * value
    tangent = jnp.tanh(value * (gelu_scale + gelu_scale * 0.044715 * square))
    half = 0.5 * value
    plus = 0.5 + 0.5 * tangent
    grad = plus + half * (1.0 - tangent * tangent) * (
        gelu_scale + gelu_scale * 3.0 * 0.044715 * square
    )
    return value * plus, grad


def column(value, c):
    return jnp.concatenate([value[r, c : c + 1] for r in range(value.shape[0])], axis=0)


def rim_kernel(canvas_ref, *out_refs):
    cols = canvas_ref.shape[1]
    begin = canvas_ref[:, 0:16, :].astype(f32)
    end = canvas_ref[:, cols - 16 :, :].astype(f32)
    for c in range(2):
        pair = column(begin, c), column(end, 14 + c)
        if len(out_refs) == 1:
            out_refs[0][c] = jnp.where(lax.axis_index("cols") == 0, pair[1], pair[0]).astype(bf16)
        else:
            out_refs[0][c], out_refs[1][c] = pair[0].astype(bf16), pair[1].astype(bf16)


def payload_kernel(canvas_ref, *refs):
    first_ref, last_ref, left_ref, right_ref = refs[-4:]
    rows, cols, width = canvas_ref.shape
    if len(refs) == 5:
        here = lax.axis_index("cols")
        other = refs[0][...].astype(f32)
        left_ref[...] = jnp.where(here == 0, 0.0, other).astype(bf16)
        right_ref[...] = jnp.where(here == 0, other, 0.0).astype(bf16)
    else:
        left_ref[...], right_ref[...] = refs[0][...], refs[1][...]
    beyond = [ref[c].astype(f32) for ref in (left_ref, right_ref) for c in range(2)]
    for ref, r in ((first_ref, 0), (last_ref, rows - 2)):
        for k in range(2):
            ref[k * cols : (k + 1) * cols, :] = canvas_ref[r + k]
        rim = [part[r + k : r + k + 1] for k in range(2) for part in beyond]
        rim = jnp.concatenate([*rim, jnp.zeros((8, width), f32)], axis=0)
        ref[2 * cols :, :] = rim.astype(bf16)


def fill_row(cat_ref, r, row, before, after):
    cols, width = row.shape
    wide = row.astype(f32)
    place = lax.broadcasted_iota(jnp.int32, (cols, width), 0)
    at = slice(r * cols, (r + 1) * cols)
    moved = jnp.where(place == 0, before, pltpu.roll(wide, 1, 0))
    cat_ref[at, 0:width] = moved.astype(bf16)
    cat_ref[at, width : 2 * width] = row.astype(bf16)
    moved = jnp.where(place == cols - 1, after, pltpu.roll(wide, cols - 1, 0))
    cat_ref[at, 2 * width : 3 * width] = moved.astype(bf16)


def gram_tiles(feat, gram_ref, base_ref=None):
    width = feat.shape[1]
    half = width // 2
    product = functools.partial(
        lax.dot_general,
        dimension_numbers=(((0,), (0,)), ((), ())),
        preferred_element_type=f32,
    )
    upper = product(feat[:, :half], feat)
    lower = product(feat[:, half:], feat[:, half:])
    for n, (i, j) in enumerate(tile_pairs(width)):
        at = slice(n * tile, (n + 1) * tile)
        if i * tile < half:
            part = upper[i * tile : (i + 1) * tile, j * tile : (j + 1) * tile]
        else:
            k, m = i * tile - half, j * tile - half
            part = lower[k : k + tile, m : m + tile]
        gram_ref[at, :] = part if base_ref is None else part + base_ref[at, :]


def inner_kernel(
    shape, own_ref, left_ref, right_ref, kernel_ref, bias_ref,
    feat_ref, slope_ref, gram_ref, row_ref, cat_ref,
):
    row_ref[...] = bias_ref[...].astype(f32).reshape(row_ref.shape)
    tile_rows, tile_cols, in_width, out_width, step = shape
    lefts, rights = left_ref[1].astype(f32), right_ref[0].astype(f32)
    for r in range(tile_rows):
        fill_row(cat_ref, r, own_ref[r], lefts[r : r + 1], rights[r : r + 1])
    bias = row_ref[...]
    root = 1.0 / math.sqrt(out_width)
    span = 3 * in_width
    for h in range(0, tile_rows - 2, step):
        total = bias
        for a in range(3):
            total = total + jnp.dot(
                cat_ref[(h + a) * tile_cols : (h + a + step) * tile_cols, :],
                kernel_ref[a * span : (a + 1) * span, :],
                preferred_element_type=f32,
            )
        features, slope = gelu_pair(total)
        at = slice(h * tile_cols, (h + step) * tile_cols)
        feat_ref[at, :] = features.astype(bf16)
        slope_ref[at, :] = (slope * root).astype(bf16)
    gram_tiles(feat_ref[...], gram_ref)


def outer_kernel(
    shape, own_ref, low_ref, high_ref, left_ref, right_ref, kernel_ref, bias_ref, base_ref,
    feat_ref, slope_ref, send_ref, keep_ref, cat_ref, edge_ref, gram_ref,
):
    tile_rows, tile_cols, in_width, out_width, step = shape
    first = (lax.axis_index("rows") > 0).astype(f32)
    last = (lax.axis_index("rows") < lax.axis_size("rows") - 1).astype(f32)
    left = (lax.axis_index("cols") > 0).astype(f32)
    right = (lax.axis_index("cols") < lax.axis_size("cols") - 1).astype(f32)
    main = 2 * tile_cols
    low_rim, high_rim = low_ref[main:, :].astype(f32), high_ref[main:, :].astype(f32)
    own_begin = column(own_ref[:, 0:16, :].astype(f32), 0)
    own_end = column(own_ref[:, tile_cols - 16 :, :].astype(f32), 15)

    def sides(c, own):
        return jnp.concatenate(
            [low_rim[c : c + 1], low_rim[4 + c : 5 + c], own, high_rim[c : c + 1], high_rim[4 + c : 5 + c]],
            axis=0,
        )

    def ends(c, own):
        c16 = c // 16 * 16
        piece = lambda ref, k: ref[k + c16 : k + c16 + 16, :].astype(f32)[c - c16 : c - c16 + 1]
        rows = [piece(low_ref, 0), piece(low_ref, tile_cols), own]
        return jnp.concatenate([*rows, piece(high_ref, 0), piece(high_ref, tile_cols)], axis=0)

    lefts = [
        sides(0, left_ref[0].astype(f32)), sides(1, left_ref[1].astype(f32)), ends(0, own_begin)
    ]
    rights = [
        ends(tile_cols - 1, own_end), sides(2, right_ref[0].astype(f32)), sides(3, right_ref[1].astype(f32))
    ]
    span = 3 * in_width
    lines = [0, 1, 2, 3, tile_rows, tile_rows + 1, tile_rows + 2, tile_rows + 3]
    for r, line in enumerate(lines):
        if line < 2:
            row = low_ref[line * tile_cols : (line + 1) * tile_cols, :]
        elif line < tile_rows + 2:
            row = own_ref[line - 2]
        else:
            k = line - tile_rows - 2
            row = high_ref[k * tile_cols : (k + 1) * tile_cols, :]
        fill_row(cat_ref, r, row, lefts[1][line : line + 1], rights[1][line : line + 1])
    blank = jnp.zeros((edge - tile_rows - 2, in_width), f32)
    for a in range(3):
        for b in range(3):
            piece = jnp.concatenate(
                [lefts[b][a : a + tile_rows + 2], blank, rights[b][a : a + tile_rows + 2], blank],
                axis=0,
            )
            at = (3 * a + b) * in_width
            edge_ref[:, at : at + in_width] = piece.astype(bf16)
    bias = bias_ref[...]
    root = 1.0 / math.sqrt(out_width)
    totals = [bias, bias, bias]
    for a in range(3):
        weights = kernel_ref[a * span : (a + 1) * span, :]
        for k in range(2):
            totals[k] = totals[k] + jnp.dot(
                cat_ref[(4 * k + a) * tile_cols : (4 * k + a + 2) * tile_cols, :],
                weights,
                preferred_element_type=f32,
            )
        totals[2] = totals[2] + jnp.dot(
            edge_ref[:, a * span : (a + 1) * span], weights, preferred_element_type=f32
        )
    for k in range(2):
        features, slope = gelu_pair(totals[k])
        slope = slope * root
        at = k * main
        feat_ref[at : at + main, :] = features.astype(bf16)
        scale = (first, 1.0) if k == 0 else (1.0, last)
        slope_ref[at : at + tile_cols, :] = (slope[:tile_cols] * scale[0]).astype(bf16)
        slope_ref[at + tile_cols : at + main, :] = (slope[tile_cols:] * scale[1]).astype(bf16)
    features, slope = gelu_pair(totals[2])
    line = lax.broadcasted_iota(jnp.int32, (2 * edge, out_width), 0)
    weight = jnp.where(line < edge, left, right)
    weight = jnp.where(line % edge == 0, weight * first, weight)
    weight = jnp.where(line % edge == tile_rows + 1, weight * last, weight)
    feat_ref[2 * main :, :] = features.astype(bf16)
    slope_ref[2 * main :, :] = (slope * root * weight).astype(bf16)
    gram_tiles(feat_ref[tile_cols : 3 * tile_cols, :], gram_ref, base_ref)
    half = send_ref.shape[0]
    side = side_of(0)
    send_ref[...] = gram_ref[rows_at(1 - side, half), :].astype(bf16)
    keep_ref[...] = gram_ref[rows_at(side, half), :]


def backward_kernel(
    shape, pixel_total, mine_ref, other_ref, target_ref, in_feat_ref, in_slope_ref, out_feat_ref, out_slope_ref,
    kernel_ref, own_gram_ref, out_ref, gram_ref, full_ref, sym_ref, cat_ref,
):
    tile_rows, tile_cols, in_width, out_width, step = shape
    half = mine_ref.shape[0]
    side = side_of(0)
    gram_ref[rows_at(side, half), :] = mine_ref[...].astype(f32)
    gram_ref[rows_at(1 - side, half), :] = other_ref[...].astype(f32)
    for n, (i, j) in enumerate(tile_pairs(out_width)):
        at_i, at_j = slice(i * tile, (i + 1) * tile), slice(j * tile, (j + 1) * tile)
        gram = gram_ref[n * tile : (n + 1) * tile, :] * (1.0 / pixel_total)
        both = 2.0 * gram - (target_ref[at_i, at_j].astype(f32) + target_ref[at_j, at_i].astype(f32).T)
        full_ref[at_i, at_j] = gram
        sym_ref[at_i, at_j] = both.astype(bf16)
        if i != j:
            full_ref[at_j, at_i] = gram.T
            sym_ref[at_j, at_i] = both.T.astype(bf16)
    share = own_gram_ref.shape[0]
    start = device_index() * share
    if share % 8 == 0:
        own_gram_ref[...] = full_ref[pl.ds(pl.multiple_of(start, 8), share), :]
    else:
        group = full_ref[pl.ds(pl.multiple_of(start // 8 * 8, 8), 8), :]
        picked = group[0:share]
        for k in range(share, 8, share):
            picked = jnp.where(start % 8 == k, group[k : k + share], picked)
        own_gram_ref[...] = picked

    def grad_of(feat_ref, slope_ref, at):
        product = jnp.dot(feat_ref[at, :], sym_ref[...], preferred_element_type=f32)
        return product * slope_ref[at, :].astype(f32)

    main = 2 * tile_cols
    edges = grad_of(out_feat_ref, out_slope_ref, slice(2 * main, None))
    lines = [
        (out_feat_ref, out_slope_ref, 0, 0),
        (out_feat_ref, out_slope_ref, main, tile_rows),
    ] + [
        (in_feat_ref, in_slope_ref, h * tile_cols, h + 2) for h in range(0, tile_rows - 2, step)
    ]
    for feat_ref, slope_ref, begin, r in lines:
        grad = grad_of(feat_ref, slope_ref, slice(begin, begin + step * tile_cols))
        for k in range(step):
            fill_row(
                cat_ref, r + k, grad[k * tile_cols : (k + 1) * tile_cols],
                edges[r + k : r + k + 1], edges[edge + r + k : edge + r + k + 1],
            )
    for h in range(0, tile_rows, step):
        total = jnp.zeros((step * tile_cols, in_width), f32)
        for a in range(3):
            for b in range(3):
                total = total + lax.dot_general(
                    cat_ref[
                        (h + 2 - a) * tile_cols : (h + 2 - a + step) * tile_cols,
                        (2 - b) * out_width : (3 - b) * out_width,
                    ],
                    kernel_ref[(3 * a + b) * in_width : (3 * a + b + 1) * in_width, :],
                    (((1,), (1,)), ((), ())),
                    preferred_element_type=f32,
                )
        out_ref[h * tile_cols : (h + step) * tile_cols, :] = total.astype(bf16)


def on_device(canvas, conv_weight, conv_bias, target_gram):
    tile_rows, tile_cols, in_width = canvas.shape
    out_width = conv_weight.shape[3]
    pixel_total = tile_rows * tile_cols * lax.axis_size("rows") * lax.axis_size("cols")
    shape = (tile_rows, tile_cols, in_width, out_width, 2)
    kernel = conv_weight.reshape(9 * in_width, out_width)
    params = pltpu.CompilerParams(vmem_limit_bytes=24 * 1024 * 1024)
    vmem = pl.BlockSpec(memory_space=pltpu.VMEM)
    packed_shape = jax.ShapeDtypeStruct((len(tile_pairs(out_width)) * tile, tile), f32)

    bits = (lax.axis_size("rows") * lax.axis_size("cols")).bit_length() - 1
    rim_shape = jax.ShapeDtypeStruct((2, tile_rows, in_width), bf16)
    two = lax.axis_size("cols") == 2
    rims = local(
        rim_kernel,
        (rim_shape,) * (1 if two else 2),
        "column_rims",
        canvas,
        cost_estimate=pl.CostEstimate(flops=4_000_000_000, bytes_accessed=600_000, transcendentals=0),
    )
    if two:
        beyond = [lax.ppermute(rims[0], "cols", [(0, 1), (1, 0)])]
    else:
        beyond = shift_cols(rims[1], rims[0])
    payload_shape = jax.ShapeDtypeStruct((2 * tile_cols + edge, in_width), bf16)
    first, last, left, right = local(
        payload_kernel, (payload_shape, payload_shape, rim_shape, rim_shape), "row_payload", canvas, *beyond
    )
    low, high = shift_rows(last, first)
    gather = Gather(target_gram.astype(bf16)[None])
    gather.step(bits - 1, first)

    inner = (tile_rows - 2) * tile_cols
    in_feat, in_slope, in_gram, bias = pl.pallas_call(
        functools.partial(inner_kernel, shape),
        out_shape=(
            jax.ShapeDtypeStruct((inner, out_width), bf16),
            jax.ShapeDtypeStruct((inner, out_width), bf16),
            packed_shape,
            jax.ShapeDtypeStruct((1, out_width), f32),
        ),
        in_specs=[vmem] * 5,
        scratch_shapes=[pltpu.VMEM((tile_rows * tile_cols, 3 * in_width), bf16)],
        compiler_params=params,
        name="inner_rows",
        cost_estimate=pl.CostEstimate(
            flops=2 * inner * (9 * in_width + out_width) * out_width,
            bytes_accessed=6_000_000,
            transcendentals=inner * out_width,
        ),
    )(canvas, left, right, kernel, conv_bias)

    outer = 4 * tile_cols + 2 * edge
    half_shape = (packed_shape.shape[0] // 2, tile)
    out_feat, out_slope, send, keep = pl.pallas_call(
        functools.partial(outer_kernel, shape),
        out_shape=(
            jax.ShapeDtypeStruct((outer, out_width), bf16),
            jax.ShapeDtypeStruct((outer, out_width), bf16),
            jax.ShapeDtypeStruct(half_shape, bf16),
            jax.ShapeDtypeStruct(half_shape, f32),
        ),
        in_specs=[vmem] * 8,
        scratch_shapes=[
            pltpu.VMEM((8 * tile_cols, 3 * in_width), bf16),
            pltpu.VMEM((2 * edge, 9 * in_width), bf16),
            pltpu.VMEM(packed_shape.shape, f32),
        ],
        compiler_params=params,
        name="outer_rows",
    )(canvas, low, high, left, right, kernel, bias, in_gram)

    rest = [bit for bit in range(bits - 2, 2, -1)]
    order = [*rest, *([None] * max(0, 2 - len(rest))), 1, 2, 0]
    mine, other, left_over = sum_all(send, keep, gather, order)
    for bit in left_over:
        gather.step(bit, other)
    target_full = gather.rows.reshape(out_width, out_width)

    own_gram, grad = pl.pallas_call(
        functools.partial(backward_kernel, shape, pixel_total),
        out_shape=(
            jax.ShapeDtypeStruct(target_gram.shape, f32),
            jax.ShapeDtypeStruct((tile_rows * tile_cols, in_width), bf16),
        ),
        in_specs=[vmem] * 8,
        scratch_shapes=[
            pltpu.VMEM(packed_shape.shape, f32),
            pltpu.VMEM((out_width, out_width), f32),
            pltpu.VMEM((out_width, out_width), bf16),
            pltpu.VMEM(((tile_rows + 2) * tile_cols, 3 * out_width), bf16),
        ],
        compiler_params=params,
        name="grad_conv",
    )(mine, other, target_full, in_feat, in_slope, out_feat, out_slope, kernel)
    return own_gram, grad.reshape(tile_rows, tile_cols, in_width)


def solution(mesh):
    return jax.shard_map(
        on_device,
        mesh=mesh,
        in_specs=(P("rows", "cols", None), P(), P(), P(("rows", "cols"), None)),
        out_specs=(P(("rows", "cols"), None), P("rows", "cols", None)),
        check_vma=False,
    )
```

profile of v0, /device:TPU:0, one launch (start us, length us, event | category | flops | bytes accessed | tf_op | source)
XLA Modules:
  0.0 61.2 jit_solution(14161370268498897954)
XLA Ops:
  0.6 1.2 %copy-done.1 = bf16[8,128,256]{2,1,0:T(8,128)(2,1)S(1)} copy-done((bf16[8,128,256]{2,1,0:T(8,128)(2,1)S(1)}, bf16[8,128,256]{2,1,0:T(8,128)(2,1)}, u32[]{:S(2)}) %copy-start.1) | copy-done | bytes 524312
  1.9 0.5 collective-permute-start
  2.4 0.8 %collective-permute-done.refs_0_ = bf16[2,8,256]{2,1,0:T(8,128)(2,1)S(1)} collective-permute-done((bf16[2,8,256]{2,1,0:T(8,128)(2,1)S(1)}, bf16[2,8,256]{2,1,0:T(8,128)(2,1)S(1)}, u32[]{:S(2)}, u32[]{:S(2)}) %collective-permute-start) | collective-permute-done | bytes 8224 | tf_op jit(solution)/shard_map/ppermute | solution.py:417
  3.2 4.7 %collective-permute-start.1 = (bf16[272,256]{1,0:T(8,128)(2,1)S(1)}, bf16[272,256]{1,0:T(8,128)(2,1)S(1)}, u32[]{:S(2)}, u32[]{:S(2)}) collective-permute-start(bf16[272,256]{1,0:T(8,128)(2,1)S(1)} %get-tuple-element.25), channel_id=1, source_target_pairs={{0,2},{2,4},{4,6},{6,8},{8,10},{10,12},{12,14},{14,16},{16,18},{18... | collective-permute-start | bytes 417800 | tf_op jit(solution)/shard_map/ppermute | solution.py:26
  8.0 1.3 %collective-permute-start.2 = (bf16[272,256]{1,0:T(8,128)(2,1)S(1)}, bf16[272,256]{1,0:T(8,128)(2,1)S(1)}, u32[]{:S(2)}, u32[]{:S(2)}) collective-permute-start(bf16[272,256]{1,0:T(8,128)(2,1)S(1)} %get-tuple-element.26), channel_id=1, source_target_pairs={{2,0},{4,2},{6,4},{8,6},{10,8},{12,10},{14,12},{16,14},{18,16},{20... | collective-permute-start | bytes 417800 | tf_op jit(solution)/shard_map/ppermute | solution.py:26
  9.3 2.8 %inner_rows.1 = (bf16[768,512]{1,0:T(8,128)(2,1)S(1)}, bf16[768,512]{1,0:T(8,128)(2,1)S(1)}, f32[1280,128]{1,0:T(8,128)S(1)}, f32[1,512]{1,0:T(1,128)S(1)}) custom-call(bf16[8,128,256]{2,1,0:T(8,128)(2,1)S(1)} %copy-done.2, bf16[2,8,256]{2,1,0:T(8,128)(2,1)S(1)} %get-tuple-element.27.left_ref, bf16[2,8,256]{2,1,0:T(8,128)(2,1)S(1)} %get-tuple-element.28.right_ref, ...), custom_call_target="tpu_custom_call" | custom-call | flops 2214592512 | bytes 6000000 | tf_op jit(solution)/shard_map/inner_rows/pallas_call | solution.py:429
  12.1 0.0 copy-start.4
  12.1 4.0 %collective-permute-done.2.high_ref = bf16[272,256]{1,0:T(8,128)(2,1)S(1)} collective-permute-done((bf16[272,256]{1,0:T(8,128)(2,1)S(1)}, bf16[272,256]{1,0:T(8,128)(2,1)S(1)}, u32[]{:S(2)}, u32[]{:S(2)}) %collective-permute-start.2) | collective-permute-done | bytes 139296 | tf_op jit(solution)/shard_map/ppermute | solution.py:26
  16.2 2.3 %outer_rows.1 = (bf16[544,512]{1,0:T(8,128)(2,1)S(1)}, bf16[544,512]{1,0:T(8,128)(2,1)S(1)}, bf16[640,128]{1,0:T(8,128)(2,1)S(1)}, f32[640,128]{1,0:T(8,128)S(1)}) custom-call(bf16[8,128,256]{2,1,0:T(8,128)(2,1)S(1)} %copy-done.2, bf16[272,256]{1,0:T(8,128)(2,1)S(1)} %collective-permute-done.1.low_ref, bf16[272,256]{1,0:T(8,128)(2,1)S(1)} %collective-permute-done.2.high_ref, ...), custom_call_target="tpu_custom_call" | custom-call | tf_op jit(solution)/shard_map/outer_rows/pallas_call | solution.py:450
  18.5 0.1 collective-permute-start.3
  18.6 1.4 %collective-permute-done.3.got_ref = bf16[640,128]{1,0:T(8,128)(2,1)S(1)} collective-permute-done((bf16[640,128]{1,0:T(8,128)(2,1)S(1)}, bf16[640,128]{1,0:T(8,128)(2,1)S(1)}, u32[]{:S(2)}, u32[]{:S(2)}) %collective-permute-start.3) | collective-permute-done | bytes 163872 | tf_op jit(solution)/shard_map/ppermute | solution.py:42
  20.0 1.6 %collective-permute-start.4 = (bf16[320,128]{1,0:T(8,128)(2,1)S(1)}, bf16[320,128]{1,0:T(8,128)(2,1)S(1)}, u32[]{:S(2)}, u32[]{:S(2)}) collective-permute-start(bf16[320,128]{1,0:T(8,128)(2,1)S(1)} %get-tuple-element.34), channel_id=1, source_target_pairs={{0,2},{1,3},{2,0},{3,1},{4,6},{5,7},{6,4},{7,5},{8,10},{9,11},{10,... | collective-permute-start | bytes 245768 | tf_op jit(solution)/shard_map/ppermute | solution.py:42
  21.6 2.6 %collective-permute-start.11 = (bf16[1,16,512]{2,1,0:T(8,128)(2,1)S(1)}, bf16[1,16,512]{2,1,0:T(8,128)(2,1)S(1)}, u32[]{:S(2)}, u32[]{:S(2)}) collective-permute-start(bf16[1,16,512]{2,1,0:T(8,128)(2,1)S(1)} %convert_bitcast_fusion), channel_id=1, source_target_pairs={{0,16},{1,17},{2,18},{3,19},{4,20},{5,21},{6,22},{7,23},{8,24},{9,... | collective-permute-start | bytes 49160 | tf_op jit(solution)/shard_map/ppermute | solution.py:42
  24.2 2.1 %collective-permute-done.11 = bf16[1,16,512]{2,1,0:T(8,128)(2,1)S(1)} collective-permute-done((bf16[1,16,512]{2,1,0:T(8,128)(2,1)S(1)}, bf16[1,16,512]{2,1,0:T(8,128)(2,1)S(1)}, u32[]{:S(2)}, u32[]{:S(2)}) %collective-permute-start.11) | collective-permute-done | bytes 16416 | tf_op jit(solution)/shard_map/ppermute | solution.py:42
  26.4 1.5 %collective-permute-start.12 = (bf16[2,16,512]{2,1,0:T(8,128)(2,1)S(1)}, bf16[2,16,512]{2,1,0:T(8,128)(2,1)S(1)}, u32[]{:S(2)}, u32[]{:S(2)}) collective-permute-start(bf16[2,16,512]{2,1,0:T(8,128)(2,1)S(1)} %bitcast.47), channel_id=1, source_target_pairs={{0,8},{1,9},{2,10},{3,11},{4,12},{5,13},{6,14},{7,15},{8,0},{9,1},... | collective-permute-start | bytes 98312 | tf_op jit(solution)/shard_map/ppermute | solution.py:42
  27.9 2.4 %collective-permute-done.12 = bf16[2,16,512]{2,1,0:T(8,128)(2,1)S(1)} collective-permute-done((bf16[2,16,512]{2,1,0:T(8,128)(2,1)S(1)}, bf16[2,16,512]{2,1,0:T(8,128)(2,1)S(1)}, u32[]{:S(2)}, u32[]{:S(2)}) %collective-permute-start.12) | collective-permute-done | bytes 32800 | tf_op jit(solution)/shard_map/ppermute | solution.py:42
  30.4 0.5 collective-permute-start.13
  30.9 2.0 %collective-permute-start.5 = (bf16[160,128]{1,0:T(8,128)(2,1)S(1)}, bf16[160,128]{1,0:T(8,128)(2,1)S(1)}, u32[]{:S(2)}, u32[]{:S(2)}) collective-permute-start(bf16[160,128]{1,0:T(8,128)(2,1)S(1)} %get-tuple-element.36), channel_id=1, source_target_pairs={{0,4},{1,5},{2,6},{3,7},{4,0},{5,1},{6,2},{7,3},{8,12},{9,13},{10,... | collective-permute-start | bytes 122888 | tf_op jit(solution)/shard_map/ppermute | solution.py:42
  32.9 2.4 %collective-permute-done.5.got_ref = bf16[160,128]{1,0:T(8,128)(2,1)S(1)} collective-permute-done((bf16[160,128]{1,0:T(8,128)(2,1)S(1)}, bf16[160,128]{1,0:T(8,128)(2,1)S(1)}, u32[]{:S(2)}, u32[]{:S(2)}) %collective-permute-start.5) | collective-permute-done | bytes 40992 | tf_op jit(solution)/shard_map/ppermute | solution.py:42
  35.4 2.0 %collective-permute-start.14 = (bf16[8,16,512]{2,1,0:T(8,128)(2,1)S(1)}, bf16[8,16,512]{2,1,0:T(8,128)(2,1)S(1)}, u32[]{:S(2)}, u32[]{:S(2)}) collective-permute-start(bf16[8,16,512]{2,1,0:T(8,128)(2,1)S(1)} %bitcast.39), channel_id=1, source_target_pairs={{0,4},{1,5},{2,6},{3,7},{4,0},{5,1},{6,2},{7,3},{8,12},{9,13},{10,... | collective-permute-start | bytes 393224 | tf_op jit(solution)/shard_map/ppermute | solution.py:42
  37.4 1.6 %collective-permute-start.6 = (bf16[160,128]{1,0:T(8,128)(2,1)S(1)}, bf16[160,128]{1,0:T(8,128)(2,1)S(1)}, u32[]{:S(2)}, u32[]{:S(2)}) collective-permute-start(bf16[160,128]{1,0:T(8,128)(2,1)S(1)} %add.3.keep_ref), channel_id=1, source_target_pairs={{0,8},{1,9},{2,10},{3,11},{4,12},{5,13},{6,14},{7,15},{8,0},{9,1},... | collective-permute-start | bytes 122888 | tf_op jit(solution)/shard_map/ppermute | solution.py:42
  39.0 2.4 %collective-permute-done.6.got_ref = bf16[160,128]{1,0:T(8,128)(2,1)S(1)} collective-permute-done((bf16[160,128]{1,0:T(8,128)(2,1)S(1)}, bf16[160,128]{1,0:T(8,128)(2,1)S(1)}, u32[]{:S(2)}, u32[]{:S(2)}) %collective-permute-start.6) | collective-permute-done | bytes 40992 | tf_op jit(solution)/shard_map/ppermute | solution.py:42
  41.4 2.7 %collective-permute-start.7 = (bf16[160,128]{1,0:T(8,128)(2,1)S(1)}, bf16[160,128]{1,0:T(8,128)(2,1)S(1)}, u32[]{:S(2)}, u32[]{:S(2)}) collective-permute-start(bf16[160,128]{1,0:T(8,128)(2,1)S(1)} %add.4.keep_ref), channel_id=1, source_target_pairs={{0,16},{1,17},{2,18},{3,19},{4,20},{5,21},{6,22},{7,23},{8,24},{9,... | collective-permute-start | bytes 122888 | tf_op jit(solution)/shard_map/ppermute | solution.py:42
  44.1 2.3 %collective-permute-done.7.got_ref = bf16[160,128]{1,0:T(8,128)(2,1)S(1)} collective-permute-done((bf16[160,128]{1,0:T(8,128)(2,1)S(1)}, bf16[160,128]{1,0:T(8,128)(2,1)S(1)}, u32[]{:S(2)}, u32[]{:S(2)}) %collective-permute-start.7) | collective-permute-done | bytes 40992 | tf_op jit(solution)/shard_map/ppermute | solution.py:42
  46.4 0.2 collective-permute-start.8
  46.6 0.1 collective-permute-start.15
  46.7 3.8 %collective-permute-done.8 = bf16[160,128]{1,0:T(8,128)(2,1)S(1)} collective-permute-done((bf16[160,128]{1,0:T(8,128)(2,1)S(1)}, bf16[160,128]{1,0:T(8,128)(2,1)S(1)}, u32[]{:S(2)}, u32[]{:S(2)}) %collective-permute-start.8) | collective-permute-done | bytes 40992 | tf_op jit(solution)/shard_map/ppermute | solution.py:42
  50.5 2.1 %collective-permute-start.9 = (bf16[320,128]{1,0:T(8,128)(2,1)S(1)}, bf16[320,128]{1,0:T(8,128)(2,1)S(1)}, u32[]{:S(2)}, u32[]{:S(2)}) collective-permute-start(bf16[320,128]{1,0:T(8,128)(2,1)S(1)} %bitcast.41), channel_id=1, source_target_pairs={{0,2},{1,3},{2,0},{3,1},{4,6},{5,7},{6,4},{7,5},{8,10},{9,11},{10,... | collective-permute-start | bytes 245768 | tf_op jit(solution)/shard_map/ppermute | solution.py:42
  52.5 2.4 %collective-permute-done.9 = bf16[320,128]{1,0:T(8,128)(2,1)S(1)} collective-permute-done((bf16[320,128]{1,0:T(8,128)(2,1)S(1)}, bf16[320,128]{1,0:T(8,128)(2,1)S(1)}, u32[]{:S(2)}, u32[]{:S(2)}) %collective-permute-start.9) | collective-permute-done | bytes 81952 | tf_op jit(solution)/shard_map/ppermute | solution.py:42
  55.0 0.1 collective-permute-start.10
  55.2 1.3 %collective-permute-done.10.other_ref = bf16[640,128]{1,0:T(8,128)(2,1)S(1)} collective-permute-done((bf16[640,128]{1,0:T(8,128)(2,1)S(1)}, bf16[640,128]{1,0:T(8,128)(2,1)S(1)}, u32[]{:S(2)}, u32[]{:S(2)}) %collective-permute-start.10) | collective-permute-done | bytes 163872 | tf_op jit(solution)/shard_map/ppermute | solution.py:42
  56.5 4.7 %grad_conv.1 = (f32[16,512]{1,0:T(8,128)}, bf16[1024,256]{1,0:T(8,128)(2,1)}) custom-call(bf16[640,128]{1,0:T(8,128)(2,1)S(1)} %bitcast.38, bf16[640,128]{1,0:T(8,128)(2,1)S(1)} %collective-permute-done.10.other_ref, bf16[512,512]{1,0:T(8,128)(2,1)S(1)} %bitcast.34, bf16[768,512]{1,0:T(8,128)(2,1)S(1)} %get-tuple-element.42.in_feat_ref, ...), custom_call_target="tpu_custom_call" | custom-call | tf_op jit(solution)/shard_map/grad_conv/pallas_call | solution.py:475
  (28 shorter events, 0.4 us)
Async XLA Ops:
  0.6 8.7 %copy-start = (bf16[3,3,256,512]{3,2,1,0:T(8,128)(2,1)S(1)}, bf16[3,3,256,512]{3,2,1,0:T(8,128)(2,1)}, u32[]{:S(2)}) copy-start(bf16[3,3,256,512]{3,2,1,0:T(8,128)(2,1)} %param.5) | copy-start | bytes 7077892
  0.6 1.2 %copy-start.1 = (bf16[8,128,256]{2,1,0:T(8,128)(2,1)S(1)}, bf16[8,128,256]{2,1,0:T(8,128)(2,1)}, u32[]{:S(2)}) copy-start(bf16[8,128,256]{2,1,0:T(8,128)(2,1)} %own_ref.3) | copy-start | bytes 1572868
  1.8 7.5 %copy-start.2 = (bf16[8,128,256]{2,1,0:T(8,128)(2,1)S(1)}, bf16[8,128,256]{2,1,0:T(8,128)(2,1)}, u32[]{:S(2)}) copy-start(bf16[8,128,256]{2,1,0:T(8,128)(2,1)} %own_ref.3) | copy-start | bytes 1572868
  1.8 7.5 %copy-start.3 = (bf16[512]{0:T(512)(128)(2,1)S(1)}, bf16[512]{0:T(512)(128)(2,1)}, u32[]{:S(2)}) copy-start(bf16[512]{0:T(512)(128)(2,1)} %bias_ref.1) | copy-start | bytes 3076
  1.9 1.3 %collective-permute-start = (bf16[2,8,256]{2,1,0:T(8,128)(2,1)S(1)}, bf16[2,8,256]{2,1,0:T(8,128)(2,1)S(1)}, u32[]{:S(2)}, u32[]{:S(2)}) collective-permute-start(bf16[2,8,256]{2,1,0:T(8,128)(2,1)S(1)} %column_rims.1), channel_id=1, source_target_pairs={{0,1},{1,0},{2,3},{3,2},{4,5},{5,4},{6,7},{7,6},{8,9},{9,8},{10,11... | collective-permute-start | bytes 24584 | tf_op jit(solution)/shard_map/ppermute | solution.py:417
  3.2 8.9 %collective-permute-start.1 = (bf16[272,256]{1,0:T(8,128)(2,1)S(1)}, bf16[272,256]{1,0:T(8,128)(2,1)S(1)}, u32[]{:S(2)}, u32[]{:S(2)}) collective-permute-start(bf16[272,256]{1,0:T(8,128)(2,1)S(1)} %get-tuple-element.25), channel_id=1, source_target_pairs={{0,2},{2,4},{4,6},{6,8},{8,10},{10,12},{12,14},{14,16},{16,18},{18... | collective-permute-start | bytes 417800 | tf_op jit(solution)/shard_map/ppermute | solution.py:26
  8.0 8.2 %collective-permute-start.2 = (bf16[272,256]{1,0:T(8,128)(2,1)S(1)}, bf16[272,256]{1,0:T(8,128)(2,1)S(1)}, u32[]{:S(2)}, u32[]{:S(2)}) collective-permute-start(bf16[272,256]{1,0:T(8,128)(2,1)S(1)} %get-tuple-element.26), channel_id=1, source_target_pairs={{2,0},{4,2},{6,4},{8,6},{10,8},{12,10},{14,12},{16,14},{18,16},{20... | collective-permute-start | bytes 417800 | tf_op jit(solution)/shard_map/ppermute | solution.py:26
  12.1 9.5 %copy-start.4 = (f32[16,512]{1,0:T(8,128)S(1)}, f32[16,512]{1,0:T(8,128)}, u32[]{:S(2)}) copy-start(f32[16,512]{1,0:T(8,128)} %param.7) | copy-start | bytes 98308
  18.5 1.5 %collective-permute-start.3 = (bf16[640,128]{1,0:T(8,128)(2,1)S(1)}, bf16[640,128]{1,0:T(8,128)(2,1)S(1)}, u32[]{:S(2)}, u32[]{:S(2)}) collective-permute-start(bf16[640,128]{1,0:T(8,128)(2,1)S(1)} %get-tuple-element.32), channel_id=1, source_target_pairs={{0,1},{1,0},{2,3},{3,2},{4,5},{5,4},{6,7},{7,6},{8,9},{9,8},{10,11... | collective-permute-start | bytes 491528 | tf_op jit(solution)/shard_map/ppermute | solution.py:42
  20.0 10.3 %collective-permute-start.4 = (bf16[320,128]{1,0:T(8,128)(2,1)S(1)}, bf16[320,128]{1,0:T(8,128)(2,1)S(1)}, u32[]{:S(2)}, u32[]{:S(2)}) collective-permute-start(bf16[320,128]{1,0:T(8,128)(2,1)S(1)} %get-tuple-element.34), channel_id=1, source_target_pairs={{0,2},{1,3},{2,0},{3,1},{4,6},{5,7},{6,4},{7,5},{8,10},{9,11},{10,... | collective-permute-start | bytes 245768 | tf_op jit(solution)/shard_map/ppermute | solution.py:42
  21.6 4.7 %collective-permute-start.11 = (bf16[1,16,512]{2,1,0:T(8,128)(2,1)S(1)}, bf16[1,16,512]{2,1,0:T(8,128)(2,1)S(1)}, u32[]{:S(2)}, u32[]{:S(2)}) collective-permute-start(bf16[1,16,512]{2,1,0:T(8,128)(2,1)S(1)} %convert_bitcast_fusion), channel_id=1, source_target_pairs={{0,16},{1,17},{2,18},{3,19},{4,20},{5,21},{6,22},{7,23},{8,24},{9,... | collective-permute-start | bytes 49160 | tf_op jit(solution)/shard_map/ppermute | solution.py:42
  26.4 3.9 %collective-permute-start.12 = (bf16[2,16,512]{2,1,0:T(8,128)(2,1)S(1)}, bf16[2,16,512]{2,1,0:T(8,128)(2,1)S(1)}, u32[]{:S(2)}, u32[]{:S(2)}) collective-permute-start(bf16[2,16,512]{2,1,0:T(8,128)(2,1)S(1)} %bitcast.47), channel_id=1, source_target_pairs={{0,8},{1,9},{2,10},{3,11},{4,12},{5,13},{6,14},{7,15},{8,0},{9,1},... | collective-permute-start | bytes 98312 | tf_op jit(solution)/shard_map/ppermute | solution.py:42
  30.4 5.0 %collective-permute-start.13 = (bf16[4,16,512]{2,1,0:T(8,128)(2,1)S(1)}, bf16[4,16,512]{2,1,0:T(8,128)(2,1)S(1)}, u32[]{:S(2)}, u32[]{:S(2)}) collective-permute-start(bf16[4,16,512]{2,1,0:T(8,128)(2,1)S(1)} %bitcast.43), channel_id=1, source_target_pairs={{0,2},{1,3},{2,0},{3,1},{4,6},{5,7},{6,4},{7,5},{8,10},{9,11},{10,... | collective-permute-start | bytes 196616 | tf_op jit(solution)/shard_map/ppermute | solution.py:42
  30.9 4.4 %collective-permute-start.5 = (bf16[160,128]{1,0:T(8,128)(2,1)S(1)}, bf16[160,128]{1,0:T(8,128)(2,1)S(1)}, u32[]{:S(2)}, u32[]{:S(2)}) collective-permute-start(bf16[160,128]{1,0:T(8,128)(2,1)S(1)} %get-tuple-element.36), channel_id=1, source_target_pairs={{0,4},{1,5},{2,6},{3,7},{4,0},{5,1},{6,2},{7,3},{8,12},{9,13},{10,... | collective-permute-start | bytes 122888 | tf_op jit(solution)/shard_map/ppermute | solution.py:42
  35.4 11.2 %collective-permute-start.14 = (bf16[8,16,512]{2,1,0:T(8,128)(2,1)S(1)}, bf16[8,16,512]{2,1,0:T(8,128)(2,1)S(1)}, u32[]{:S(2)}, u32[]{:S(2)}) collective-permute-start(bf16[8,16,512]{2,1,0:T(8,128)(2,1)S(1)} %bitcast.39), channel_id=1, source_target_pairs={{0,4},{1,5},{2,6},{3,7},{4,0},{5,1},{6,2},{7,3},{8,12},{9,13},{10,... | collective-permute-start | bytes 393224 | tf_op jit(solution)/shard_map/ppermute | solution.py:42
  37.4 4.0 %collective-permute-start.6 = (bf16[160,128]{1,0:T(8,128)(2,1)S(1)}, bf16[160,128]{1,0:T(8,128)(2,1)S(1)}, u32[]{:S(2)}, u32[]{:S(2)}) collective-permute-start(bf16[160,128]{1,0:T(8,128)(2,1)S(1)} %add.3.keep_ref), channel_id=1, source_target_pairs={{0,8},{1,9},{2,10},{3,11},{4,12},{5,13},{6,14},{7,15},{8,0},{9,1},... | collective-permute-start | bytes 122888 | tf_op jit(solution)/shard_map/ppermute | solution.py:42
  41.4 5.0 %collective-permute-start.7 = (bf16[160,128]{1,0:T(8,128)(2,1)S(1)}, bf16[160,128]{1,0:T(8,128)(2,1)S(1)}, u32[]{:S(2)}, u32[]{:S(2)}) collective-permute-start(bf16[160,128]{1,0:T(8,128)(2,1)S(1)} %add.4.keep_ref), channel_id=1, source_target_pairs={{0,16},{1,17},{2,18},{3,19},{4,20},{5,21},{6,22},{7,23},{8,24},{9,... | collective-permute-start | bytes 122888 | tf_op jit(solution)/shard_map/ppermute | solution.py:42
  46.4 4.1 %collective-permute-start.8 = (bf16[160,128]{1,0:T(8,128)(2,1)S(1)}, bf16[160,128]{1,0:T(8,128)(2,1)S(1)}, u32[]{:S(2)}, u32[]{:S(2)}) collective-permute-start(bf16[160,128]{1,0:T(8,128)(2,1)S(1)} %add.5), channel_id=1, source_target_pairs={{0,4},{1,5},{2,6},{3,7},{4,0},{5,1},{6,2},{7,3},{8,12},{9,13},{10,... | collective-permute-start | bytes 122888 | tf_op jit(solution)/shard_map/ppermute | solution.py:42
  46.6 8.5 %collective-permute-start.15 = (bf16[16,16,512]{2,1,0:T(8,128)(2,1)S(1)}, bf16[16,16,512]{2,1,0:T(8,128)(2,1)S(1)}, u32[]{:S(2)}, u32[]{:S(2)}) collective-permute-start(bf16[16,16,512]{2,1,0:T(8,128)(2,1)S(1)} %bitcast.35), channel_id=1, source_target_pairs={{0,1},{1,0},{2,3},{3,2},{4,5},{5,4},{6,7},{7,6},{8,9},{9,8},{10,11... | collective-permute-start | bytes 786440 | tf_op jit(solution)/shard_map/ppermute | solution.py:42
  50.5 4.5 %collective-permute-start.9 = (bf16[320,128]{1,0:T(8,128)(2,1)S(1)}, bf16[320,128]{1,0:T(8,128)(2,1)S(1)}, u32[]{:S(2)}, u32[]{:S(2)}) collective-permute-start(bf16[320,128]{1,0:T(8,128)(2,1)S(1)} %bitcast.41), channel_id=1, source_target_pairs={{0,2},{1,3},{2,0},{3,1},{4,6},{5,7},{6,4},{7,5},{8,10},{9,11},{10,... | collective-permute-start | bytes 245768 | tf_op jit(solution)/shard_map/ppermute | solution.py:42
  55.0 1.5 %collective-permute-start.10 = (bf16[640,128]{1,0:T(8,128)(2,1)S(1)}, bf16[640,128]{1,0:T(8,128)(2,1)S(1)}, u32[]{:S(2)}, u32[]{:S(2)}) collective-permute-start(bf16[640,128]{1,0:T(8,128)(2,1)S(1)} %bitcast.37), channel_id=1, source_target_pairs={{0,1},{1,0},{2,3},{3,2},{4,5},{5,4},{6,7},{7,6},{8,9},{9,8},{10,11... | collective-permute-start | bytes 491528 | tf_op jit(solution)/shard_map/ppermute | solution.py:42
where the time goes:
time: 61.3 us; the launch traced here: 61.2 us
  waiting for transfers between devices  25.4 us (41%)
  starting transfers between devices  23.6 us (38%)
  Pallas kernels  10.1 us (16%)
  local copies, waits for them, and re-layouts  1.2 us (2%)
  between operations  0.84 us (1%)
    ppermute x13, waiting for transfers between devices, swap(): lax.ppermute(value, ('rows', 'cols'), [(i, i ^ 1 << bit) for i in range(t...  20.6 us
    ppermute x13, starting transfers between devices, swap(): lax.ppermute(value, ('rows', 'cols'), [(i, i ^ 1 << bit) for i in range(t...  17 us
    ppermute x1, starting transfers between devices, shift_rows(): lax.ppermute(last, 'rows', forward)  4.74 us
    pallas_call x1, Pallas kernels, on_device(): pl.pallas_call(functools.partial(backward_kernel, shape, pixel_total), ou...  4.68 us
    ppermute x1, waiting for transfers between devices, shift_rows(): lax.ppermute(first, 'rows', backward)  4.02 us
    pallas_call x1, Pallas kernels, on_device(): pl.pallas_call(functools.partial(inner_kernel, shape), out_shape=(jax.Sha...  2.78 us
    pallas_call x1, Pallas kernels, on_device(): pl.pallas_call(functools.partial(outer_kernel, shape), out_shape=(jax.Sha...  2.35 us
    ppermute x1, starting transfers between devices, shift_rows(): lax.ppermute(first, 'rows', backward)  1.29 us
  transfers between devices with their start and end apart: 16, of which 11 were waited for; matrix products, arithmetic and copies ran while one was open for 0% of the time, Pallas kernels for 5%

commit v1 on v0

--- a/solution.py
+++ b/solution.py
@@ -19,11 +19,9 @@
     return [(i, j) for i in range(count) for j in range(i, count)]
 
 
-def shift_rows(last, first):
-    count = lax.axis_size("rows")
-    forward = [(i, i + 1) for i in range(count - 1)]
-    backward = [(target, source) for source, target in forward]
-    return lax.ppermute(last, "rows", forward), lax.ppermute(first, "rows", backward)
+def swap_rows(pairs, values):
+    perm = lambda low: [(i, i + 1) for i in low] + [(i + 1, i) for i in low]
+    return [lax.ppermute(value, "rows", perm(low)) for low, value in zip(pairs, values)]
 
 
 def shift_cols(last, first):
@@ -37,9 +35,16 @@
     return lax.axis_index("rows") * lax.axis_size("cols") + lax.axis_index("cols")
 
 
-def swap(value, bit):
+def swap(value, bit, core=None):
     total = lax.axis_size("rows") * lax.axis_size("cols")
-    return lax.ppermute(value, ("rows", "cols"), [(i, i ^ (1 << bit)) for i in range(total)])
+    perm = [(i, i ^ (1 << bit)) for i in range(total) if core is None or i % 2 == core]
+    return lax.ppermute(value, ("rows", "cols"), perm)
+
+
+def hand_over(value, core):
+    total = lax.axis_size("rows") * lax.axis_size("cols")
+    perm = [(i, i ^ 1) for i in range(total) if i % 2 == core]
+    return lax.ppermute(value, ("rows", "cols"), perm)
 
 
 def local(body, out_shape, name, *operands, **kwargs):
@@ -97,43 +102,38 @@
     return local(body, jax.ShapeDtypeStruct(shape, mine.dtype), "join", mine, other)
 
 
-class Gather:
-    def __init__(self, rows):
-        self.rows, self.done = rows, []
-
-    def step(self, bit, after):
-        share = self.rows.shape[-2:]
-        send, _ = lax.optimization_barrier((self.rows, after))
-        got = swap(send, bit)
-        lead = 1 << sum(other > bit for other in self.done)
-        parts = [part.reshape(lead, -1, *share) for part in (send, got)]
-        self.rows = join(*parts, bit).reshape(-1, *share)
-        self.done.append(bit)
-
-
-def sum_all(send, keep, gather, order):
+def gather_step(rows, bit, after, core=None):
+    share = rows.shape[-2:]
+    send, _ = lax.optimization_barrier((rows, after))
+    got = swap(send, bit, core)
+    lead = max(1, rows.shape[0] // 2)
+    return join(send.reshape(lead, -1, *share), got.reshape(lead, -1, *share), bit).reshape(-1, *share)
+
+
+def sum_all(send, keep, rows):
     bits = (lax.axis_size("rows") * lax.axis_size("cols")).bit_length() - 1
-    halving = list(range(min(3, bits)))
-    order = list(order)
+    halving = list(range(1, min(3, bits)))
+    order = list(reversed(range(1, bits)))
 
     def step(value, bit):
-        beside = order.pop(0) if order else None
-        got = swap(value, bit)
-        if beside is not None:
-            gather.step(beside, value)
+        nonlocal rows
+        got = swap(value, bit, 1)
+        if order:
+            rows = gather_step(rows, order.pop(0), value, 0)
         return got
 
-    got = step(send, 0)
-    for bit in halving[1:]:
+    got = hand_over(send, 0)
+    for bit in halving:
         send, keep = halve(keep, got, bit)
         got = step(send, bit)
     mine = add(keep, got)
-    for bit in range(len(halving), bits):
+    for bit in range(len(halving) + 1, bits):
         mine = add(mine, step(mine, bit))
-    for bit in reversed(halving[1:]):
-        got = step(mine, bit)
-        mine = join(mine[None], got[None], bit).reshape(-1, mine.shape[1])
-    return mine, step(mine, 0), order
+    for bit in reversed(halving):
+        before = mine
+        mine = join(mine[None], step(mine, bit)[None], bit).reshape(-1, mine.shape[1])
+    rows, _ = lax.optimization_barrier((rows, before))
+    return mine, hand_over(mine, 1), rows, hand_over(rows, 0)
 
 
 def gelu_pair(value):
@@ -163,10 +163,11 @@
             out_refs[0][c], out_refs[1][c] = pair[0].astype(bf16), pair[1].astype(bf16)
 
 
-def payload_kernel(canvas_ref, *refs):
-    first_ref, last_ref, left_ref, right_ref = refs[-4:]
+def payload_kernel(canvas_ref, target_ref, *refs):
+    even_ref, odd_ref, left_ref, right_ref, half_ref = refs[-5:]
     rows, cols, width = canvas_ref.shape
-    if len(refs) == 5:
+    half_ref[0] = target_ref[...].astype(bf16)
+    if len(refs) == 6:
         here = lax.axis_index("cols")
         other = refs[0][...].astype(f32)
         left_ref[...] = jnp.where(here == 0, 0.0, other).astype(bf16)
@@ -174,12 +175,25 @@
     else:
         left_ref[...], right_ref[...] = refs[0][...], refs[1][...]
     beyond = [ref[c].astype(f32) for ref in (left_ref, right_ref) for c in range(2)]
-    for ref, r in ((first_ref, 0), (last_ref, rows - 2)):
+
+    def fill(ref, r):
         for k in range(2):
             ref[k * cols : (k + 1) * cols, :] = canvas_ref[r + k]
         rim = [part[r + k : r + k + 1] for k in range(2) for part in beyond]
         rim = jnp.concatenate([*rim, jnp.zeros((8, width), f32)], axis=0)
         ref[2 * cols :, :] = rim.astype(bf16)
+
+    odd = lax.rem(lax.axis_index("rows"), 2)
+
+    @pl.when(odd == 0)
+    def _():
+        fill(even_ref, rows - 2)
+        fill(odd_ref, 0)
+
+    @pl.when(odd == 1)
+    def _():
+        fill(even_ref, 0)
+        fill(odd_ref, rows - 2)
 
 
 def fill_row(cat_ref, r, row, before, after):
@@ -242,10 +256,13 @@
 
 
 def outer_kernel(
-    shape, own_ref, low_ref, high_ref, left_ref, right_ref, kernel_ref, bias_ref, base_ref,
-    feat_ref, slope_ref, send_ref, keep_ref, cat_ref, edge_ref, gram_ref,
+    shape, own_ref, even_ref, odd_ref, left_ref, right_ref, kernel_ref, bias_ref, base_ref,
+    feat_ref, slope_ref, send_ref, keep_ref, cat_ref, edge_ref, low_ref, high_ref,
 ):
     tile_rows, tile_cols, in_width, out_width, step = shape
+    odd = lax.rem(lax.axis_index("rows"), 2)
+    low_ref[...] = jnp.where(odd == 0, odd_ref[...], even_ref[...])
+    high_ref[...] = jnp.where(odd == 0, even_ref[...], odd_ref[...])
     first = (lax.axis_index("rows") > 0).astype(f32)
     last = (lax.axis_index("rows") < lax.axis_size("rows") - 1).astype(f32)
     left = (lax.axis_index("cols") > 0).astype(f32)
@@ -322,25 +339,21 @@
     weight = jnp.where(line % edge == tile_rows + 1, weight * last, weight)
     feat_ref[2 * main :, :] = features.astype(bf16)
     slope_ref[2 * main :, :] = (slope * root * weight).astype(bf16)
-    gram_tiles(feat_ref[tile_cols : 3 * tile_cols, :], gram_ref, base_ref)
-    half = send_ref.shape[0]
-    side = side_of(0)
-    send_ref[...] = gram_ref[rows_at(1 - side, half), :].astype(bf16)
-    keep_ref[...] = gram_ref[rows_at(side, half), :]
+    gram_tiles(feat_ref[tile_cols : 3 * tile_cols, :], keep_ref, base_ref)
+    send_ref[...] = keep_ref[...].astype(bf16)
 
 
 def backward_kernel(
-    shape, pixel_total, mine_ref, other_ref, target_ref, in_feat_ref, in_slope_ref, out_feat_ref, out_slope_ref,
-    kernel_ref, own_gram_ref, out_ref, gram_ref, full_ref, sym_ref, cat_ref,
+    shape, pixel_total, mine_ref, other_ref, rows_ref, other_rows_ref, in_feat_ref, in_slope_ref, out_feat_ref, out_slope_ref,
+    kernel_ref, own_gram_ref, out_ref, target_ref, full_ref, sym_ref, cat_ref,
 ):
     tile_rows, tile_cols, in_width, out_width, step = shape
-    half = mine_ref.shape[0]
-    side = side_of(0)
-    gram_ref[rows_at(side, half), :] = mine_ref[...].astype(f32)
-    gram_ref[rows_at(1 - side, half), :] = other_ref[...].astype(f32)
+    core = side_of(0)
+    target_ref[...] = jnp.where(core == 0, rows_ref[...], other_rows_ref[...])
     for n, (i, j) in enumerate(tile_pairs(out_width)):
         at_i, at_j = slice(i * tile, (i + 1) * tile), slice(j * tile, (j + 1) * tile)
-        gram = gram_ref[n * tile : (n + 1) * tile, :] * (1.0 / pixel_total)
+        at = slice(n * tile, (n + 1) * tile)
+        gram = jnp.where(core == 1, mine_ref[at, :], other_ref[at, :]).astype(f32) * (1.0 / pixel_total)
         both = 2.0 * gram - (target_ref[at_i, at_j].astype(f32) + target_ref[at_j, at_i].astype(f32).T)
         full_ref[at_i, at_j] = gram
         sym_ref[at_i, at_j] = both.astype(bf16)
@@ -403,7 +416,6 @@
     vmem = pl.BlockSpec(memory_space=pltpu.VMEM)
     packed_shape = jax.ShapeDtypeStruct((len(tile_pairs(out_width)) * tile, tile), f32)
 
-    bits = (lax.axis_size("rows") * lax.axis_size("cols")).bit_length() - 1
     rim_shape = jax.ShapeDtypeStruct((2, tile_rows, in_width), bf16)
     two = lax.axis_size("cols") == 2
     rims = local(
@@ -418,12 +430,18 @@
     else:
         beyond = shift_cols(rims[1], rims[0])
     payload_shape = jax.ShapeDtypeStruct((2 * tile_cols + edge, in_width), bf16)
-    first, last, left, right = local(
-        payload_kernel, (payload_shape, payload_shape, rim_shape, rim_shape), "row_payload", canvas, *beyond
+    half_shape = jax.ShapeDtypeStruct((1, *target_gram.shape), bf16)
+    even, odd, left, right, rows = local(
+        payload_kernel,
+        (payload_shape, payload_shape, rim_shape, rim_shape, half_shape),
+        "row_payload",
+        canvas,
+        target_gram,
+        *beyond,
     )
-    low, high = shift_rows(last, first)
-    gather = Gather(target_gram.astype(bf16)[None])
-    gather.step(bits - 1, first)
+    count = lax.axis_size("rows")
+    even, odd = swap_rows([range(0, count - 1, 2), range(1, count - 1, 2)], [even, odd])
+    rows = gather_step(rows, 0, left)
 
     inner = (tile_rows - 2) * tile_cols
     in_feat, in_slope, in_gram, bias = pl.pallas_call(
@@ -445,32 +463,29 @@
         ),
     )(canvas, left, right, kernel, conv_bias)
 
+    in_gram, rows = lax.optimization_barrier((in_gram, rows))
     outer = 4 * tile_cols + 2 * edge
-    half_shape = (packed_shape.shape[0] // 2, tile)
     out_feat, out_slope, send, keep = pl.pallas_call(
         functools.partial(outer_kernel, shape),
         out_shape=(
             jax.ShapeDtypeStruct((outer, out_width), bf16),
             jax.ShapeDtypeStruct((outer, out_width), bf16),
-            jax.ShapeDtypeStruct(half_shape, bf16),
-            jax.ShapeDtypeStruct(half_shape, f32),
+            jax.ShapeDtypeStruct(packed_shape.shape, bf16),
+            packed_shape,
         ),
         in_specs=[vmem] * 8,
         scratch_shapes=[
             pltpu.VMEM((8 * tile_cols, 3 * in_width), bf16),
             pltpu.VMEM((2 * edge, 9 * in_width), bf16),
-            pltpu.VMEM(packed_shape.shape, f32),
+            pltpu.VMEM(payload_shape.shape, bf16),
+            pltpu.VMEM(payload_shape.shape, bf16),
         ],
         compiler_params=params,
         name="outer_rows",
-    )(canvas, low, high, left, right, kernel, bias, in_gram)
-
-    rest = [bit for bit in range(bits - 2, 2, -1)]
-    order = [*rest, *([None] * max(0, 2 - len(rest))), 1, 2, 0]
-    mine, other, left_over = sum_all(send, keep, gather, order)
-    for bit in left_over:
-        gather.step(bit, other)
-    target_full = gather.rows.reshape(out_width, out_width)
+    )(canvas, even, odd, left, right, kernel, bias, in_gram)
+
+    mine, other, rows, other_rows = sum_all(send, keep, rows)
+    rows, other_rows = (part.reshape(out_width, out_width) for part in (rows, other_rows))
 
     own_gram, grad = pl.pallas_call(
         functools.partial(backward_kernel, shape, pixel_total),
@@ -478,16 +493,16 @@
             jax.ShapeDtypeStruct(target_gram.shape, f32),
             jax.ShapeDtypeStruct((tile_rows * tile_cols, in_width), bf16),
         ),
-        in_specs=[vmem] * 8,
+        in_specs=[vmem] * 9,
         scratch_shapes=[
-            pltpu.VMEM(packed_shape.shape, f32),
+            pltpu.VMEM((out_width, out_width), bf16),
             pltpu.VMEM((out_width, out_width), f32),
             pltpu.VMEM((out_width, out_width), bf16),
             pltpu.VMEM(((tile_rows + 2) * tile_cols, 3 * out_width), bf16),
         ],
         compiler_params=params,
         name="grad_conv",
-    )(mine, other, target_full, in_feat, in_slope, out_feat, out_slope, kernel)
+    )(mine, other, rows, other_rows, in_feat, in_slope, out_feat, out_slope, kernel)
     return own_gram, grad.reshape(tile_rows, tile_cols, in_width)
 
 

time: 61.3 us -> 64.9 us (1.059)
  starting transfers between devices: 23.6 us -> 33.2 us
  waiting for transfers between devices: 25.4 us -> 19.2 us
    ppermute x15 -> x16, starting transfers between devices: 23.1 us -> 32.6 us  [the longest x11 23.2 us: swap(): return lax.ppermute(value, ('rows', 'cols'), perm)]
    ppermute x15 -> x16, waiting for transfers between devices: 24.6 us -> 18.4 us  [the longest x11 10.7 us: swap(): return lax.ppermute(value, ('rows', 'cols'), perm)]
  transfers between devices with their start and end apart: 16 -> 17, of which waited for: 11 -> 8; matrix products, arithmetic and copies ran while one was open for 0% -> 0% of each run, Pallas kernels for 5% -> 5%
where the time goes in v1:
time: 64.9 us; the launch traced here: 64.5 us
  starting transfers between devices  33.2 us (51%)
  waiting for transfers between devices  19.2 us (30%)
  Pallas kernels  10.1 us (16%)
  local copies, waits for them, and re-layouts  1.05 us (2%)
  between operations  0.94 us (1%)
    ppermute x11, starting transfers between devices, swap(): return lax.ppermute(value, ('rows', 'cols'), perm)  23.2 us
    ppermute x11, waiting for transfers between devices, swap(): return lax.ppermute(value, ('rows', 'cols'), perm)  10.7 us
    ppermute x3, waiting for transfers between devices, hand_over(): return lax.ppermute(value, ('rows', 'cols'), perm)  7.04 us
    ppermute x3, starting transfers between devices, hand_over(): return lax.ppermute(value, ('rows', 'cols'), perm)  6.16 us
    pallas_call x1, Pallas kernels, on_device(): pl.pallas_call(functools.partial(backward_kernel, shape, pixel_total), ou...  4.6 us
    ppermute x2, starting transfers between devices, swap_rows(): lax.ppermute(value, 'rows', perm(low))  3.31 us
    pallas_call x1, Pallas kernels, on_device(): pl.pallas_call(functools.partial(inner_kernel, shape), out_shape=(jax.Sha...  2.8 us
    pallas_call x1, Pallas kernels, on_device(): pl.pallas_call(functools.partial(outer_kernel, shape), out_shape=(jax.Sha...  2.29 us
  transfers between devices with their start and end apart: 17, of which 8 were waited for; matrix products, arithmetic and copies ran while one was open for 0% of the time, Pallas kernels for 5%

profile of v1, /device:TPU:0, one launch (start us, length us, event | category | flops | bytes accessed | tf_op | source)
XLA Modules:
  0.0 64.5 jit_solution(4607905512069340427)
XLA Ops:
  0.6 1.0 %copy-done.1 = bf16[8,128,256]{2,1,0:T(8,128)(2,1)S(1)} copy-done((bf16[8,128,256]{2,1,0:T(8,128)(2,1)S(1)}, bf16[8,128,256]{2,1,0:T(8,128)(2,1)}, u32[]{:S(2)}) %copy-start.1) | copy-done | bytes 524312
  1.7 0.5 collective-permute-start
  2.2 0.8 %collective-permute-done.refs_0_ = bf16[2,8,256]{2,1,0:T(8,128)(2,1)S(1)} collective-permute-done((bf16[2,8,256]{2,1,0:T(8,128)(2,1)S(1)}, bf16[2,8,256]{2,1,0:T(8,128)(2,1)S(1)}, u32[]{:S(2)}, u32[]{:S(2)}) %collective-permute-start) | collective-permute-done | bytes 8224 | tf_op jit(solution)/shard_map/ppermute | solution.py:429
  3.1 0.4 collective-permute-start.3
  3.5 2.7 %collective-permute-start.1 = (bf16[272,256]{1,0:T(8,128)(2,1)S(1)}, bf16[272,256]{1,0:T(8,128)(2,1)S(1)}, u32[]{:S(2)}, u32[]{:S(2)}) collective-permute-start(bf16[272,256]{1,0:T(8,128)(2,1)S(1)} %get-tuple-element.29), channel_id=1, source_target_pairs={{0,2},{4,6},{8,10},{12,14},{16,18},{20,22},{24,26},{28,30},{2,0},{... | collective-permute-start | bytes 417800 | tf_op jit(solution)/shard_map/ppermute | solution.py:24
  6.2 0.7 %collective-permute-start.2 = (bf16[272,256]{1,0:T(8,128)(2,1)S(1)}, bf16[272,256]{1,0:T(8,128)(2,1)S(1)}, u32[]{:S(2)}, u32[]{:S(2)}) collective-permute-start(bf16[272,256]{1,0:T(8,128)(2,1)S(1)} %get-tuple-element.30), channel_id=1, source_target_pairs={{2,4},{6,8},{10,12},{14,16},{18,20},{22,24},{26,28},{4,2},{8,6},{1... | collective-permute-start | bytes 417800 | tf_op jit(solution)/shard_map/ppermute | solution.py:24
  6.9 2.8 %inner_rows.1 = (bf16[768,512]{1,0:T(8,128)(2,1)S(1)}, bf16[768,512]{1,0:T(8,128)(2,1)S(1)}, f32[1280,128]{1,0:T(8,128)S(1)}, f32[1,512]{1,0:T(1,128)S(1)}) custom-call(bf16[8,128,256]{2,1,0:T(8,128)(2,1)S(1)} %copy-done.2, bf16[2,8,256]{2,1,0:T(8,128)(2,1)S(1)} %get-tuple-element.31.left_ref, bf16[2,8,256]{2,1,0:T(8,128)(2,1)S(1)} %get-tuple-element.32.right_ref, ...), custom_call_target="tpu_custom_call" | custom-call | flops 2214592512 | bytes 6000000 | tf_op jit(solution)/shard_map/inner_rows/pallas_call | solution.py:447
  9.7 0.6 collective-permute-done.1.even_ref
  10.3 0.0 collective-permute-done.2.odd_ref
  10.3 2.3 %outer_rows.1 = (bf16[544,512]{1,0:T(8,128)(2,1)S(1)}, bf16[544,512]{1,0:T(8,128)(2,1)S(1)}, bf16[1280,128]{1,0:T(8,128)(2,1)S(1)}, f32[1280,128]{1,0:T(8,128)S(1)}) custom-call(bf16[8,128,256]{2,1,0:T(8,128)(2,1)S(1)} %copy-done.2, bf16[272,256]{1,0:T(8,128)(2,1)S(1)} %collective-permute-done.1.even_ref, ...), custom_call_target="tpu_custom_call" | custom-call | tf_op jit(solution)/shard_map/outer_rows/pallas_call | solution.py:468
  12.6 1.8 %collective-permute-start.4 = (bf16[1280,128]{1,0:T(8,128)(2,1)S(1)}, bf16[1280,128]{1,0:T(8,128)(2,1)S(1)}, u32[]{:S(2)}, u32[]{:S(2)}) collective-permute-start(bf16[1280,128]{1,0:T(8,128)(2,1)S(1)} %get-tuple-element.39), channel_id=1, source_target_pairs={{0,1},{2,3},{4,5},{6,7},{8,9},{10,11},{12,13},{14,15},{16,17},{18,... | collective-permute-start | bytes 983048 | tf_op jit(solution)/shard_map/ppermute | solution.py:47
  14.4 1.2 %collective-permute-done.4.got_ref = bf16[1280,128]{1,0:T(8,128)(2,1)S(1)} collective-permute-done((bf16[1280,128]{1,0:T(8,128)(2,1)S(1)}, bf16[1280,128]{1,0:T(8,128)(2,1)S(1)}, u32[]{:S(2)}, u32[]{:S(2)}) %collective-permute-start.4) | collective-permute-done | bytes 327712 | tf_op jit(solution)/shard_map/ppermute | solution.py:47
  15.7 0.1 halve.2
  15.7 0.7 %collective-permute-start.5 = (bf16[640,128]{1,0:T(8,128)(2,1)S(1)}, bf16[640,128]{1,0:T(8,128)(2,1)S(1)}, u32[]{:S(2)}, u32[]{:S(2)}) collective-permute-start(bf16[640,128]{1,0:T(8,128)(2,1)S(1)} %get-tuple-element.41), channel_id=1, source_target_pairs={{1,3},{3,1},{5,7},{7,5},{9,11},{11,9},{13,15},{15,13},{17,19},{19,... | collective-permute-start | bytes 491528 | tf_op jit(solution)/shard_map/ppermute | solution.py:41
  16.4 9.2 %collective-permute-start.12 = (bf16[2,16,512]{2,1,0:T(8,128)(2,1)S(1)}, bf16[2,16,512]{2,1,0:T(8,128)(2,1)S(1)}, u32[]{:S(2)}, u32[]{:S(2)}) collective-permute-start(bf16[2,16,512]{2,1,0:T(8,128)(2,1)S(1)} %bitcast.44), channel_id=1, source_target_pairs={{0,16},{2,18},{4,20},{6,22},{8,24},{10,26},{12,28},{14,30},{16,0},... | collective-permute-start | bytes 98312 | tf_op jit(solution)/shard_map/ppermute | solution.py:41
  25.6 0.7 %collective-permute-start.6 = (bf16[320,128]{1,0:T(8,128)(2,1)S(1)}, bf16[320,128]{1,0:T(8,128)(2,1)S(1)}, u32[]{:S(2)}, u32[]{:S(2)}) collective-permute-start(bf16[320,128]{1,0:T(8,128)(2,1)S(1)} %get-tuple-element.43), channel_id=1, source_target_pairs={{1,5},{3,7},{5,1},{7,3},{9,13},{11,15},{13,9},{15,11},{17,21},{19,... | collective-permute-start | bytes 245768 | tf_op jit(solution)/shard_map/ppermute | solution.py:41
  26.3 1.1 %collective-permute-done.12 = bf16[2,16,512]{2,1,0:T(8,128)(2,1)S(1)} collective-permute-done((bf16[2,16,512]{2,1,0:T(8,128)(2,1)S(1)}, bf16[2,16,512]{2,1,0:T(8,128)(2,1)S(1)}, u32[]{:S(2)}, u32[]{:S(2)}) %collective-permute-start.12) | collective-permute-done | bytes 32800 | tf_op jit(solution)/shard_map/ppermute | solution.py:41
  27.5 3.8 %collective-permute-start.13 = (bf16[4,16,512]{2,1,0:T(8,128)(2,1)S(1)}, bf16[4,16,512]{2,1,0:T(8,128)(2,1)S(1)}, u32[]{:S(2)}, u32[]{:S(2)}) collective-permute-start(bf16[4,16,512]{2,1,0:T(8,128)(2,1)S(1)} %bitcast.40), channel_id=1, source_target_pairs={{0,8},{2,10},{4,12},{6,14},{8,0},{10,2},{12,4},{14,6},{16,24},{18,... | collective-permute-start | bytes 196616 | tf_op jit(solution)/shard_map/ppermute | solution.py:41
  31.3 2.3 %collective-permute-done.13 = bf16[4,16,512]{2,1,0:T(8,128)(2,1)S(1)} collective-permute-done((bf16[4,16,512]{2,1,0:T(8,128)(2,1)S(1)}, bf16[4,16,512]{2,1,0:T(8,128)(2,1)S(1)}, u32[]{:S(2)}, u32[]{:S(2)}) %collective-permute-start.13) | collective-permute-done | bytes 65568 | tf_op jit(solution)/shard_map/ppermute | solution.py:41
  33.7 2.9 %collective-permute-start.14 = (bf16[8,16,512]{2,1,0:T(8,128)(2,1)S(1)}, bf16[8,16,512]{2,1,0:T(8,128)(2,1)S(1)}, u32[]{:S(2)}, u32[]{:S(2)}) collective-permute-start(bf16[8,16,512]{2,1,0:T(8,128)(2,1)S(1)} %bitcast.37), channel_id=1, source_target_pairs={{0,4},{2,6},{4,0},{6,2},{8,12},{10,14},{12,8},{14,10},{16,20},{18,... | collective-permute-start | bytes 393224 | tf_op jit(solution)/shard_map/ppermute | solution.py:41
  36.5 0.7 %collective-permute-start.7 = (bf16[320,128]{1,0:T(8,128)(2,1)S(1)}, bf16[320,128]{1,0:T(8,128)(2,1)S(1)}, u32[]{:S(2)}, u32[]{:S(2)}) collective-permute-start(bf16[320,128]{1,0:T(8,128)(2,1)S(1)} %add.3.keep_ref), channel_id=1, source_target_pairs={{1,9},{3,11},{5,13},{7,15},{9,1},{11,3},{13,5},{15,7},{17,25},{19,... | collective-permute-start | bytes 245768 | tf_op jit(solution)/shard_map/ppermute | solution.py:41
  37.3 3.3 %collective-permute-done.14 = bf16[8,16,512]{2,1,0:T(8,128)(2,1)S(1)} collective-permute-done((bf16[8,16,512]{2,1,0:T(8,128)(2,1)S(1)}, bf16[8,16,512]{2,1,0:T(8,128)(2,1)S(1)}, u32[]{:S(2)}, u32[]{:S(2)}) %collective-permute-start.14) | collective-permute-done | bytes 131104 | tf_op jit(solution)/shard_map/ppermute | solution.py:41
  40.6 2.9 %collective-permute-start.15 = (bf16[16,16,512]{2,1,0:T(8,128)(2,1)S(1)}, bf16[16,16,512]{2,1,0:T(8,128)(2,1)S(1)}, u32[]{:S(2)}, u32[]{:S(2)}) collective-permute-start(bf16[16,16,512]{2,1,0:T(8,128)(2,1)S(1)} %bitcast.32), channel_id=1, source_target_pairs={{0,2},{2,0},{4,6},{6,4},{8,10},{10,8},{12,14},{14,12},{16,18},{18,... | collective-permute-start | bytes 786440 | tf_op jit(solution)/shard_map/ppermute | solution.py:41
  43.5 0.7 %collective-permute-start.8 = (bf16[320,128]{1,0:T(8,128)(2,1)S(1)}, bf16[320,128]{1,0:T(8,128)(2,1)S(1)}, u32[]{:S(2)}, u32[]{:S(2)}) collective-permute-start(bf16[320,128]{1,0:T(8,128)(2,1)S(1)} %add.4.keep_ref), channel_id=1, source_target_pairs={{1,17},{3,19},{5,21},{7,23},{9,25},{11,27},{13,29},{15,31},{17,1},... | collective-permute-start | bytes 245768 | tf_op jit(solution)/shard_map/ppermute | solution.py:41
  44.2 0.7 %collective-permute-start.9 = (bf16[320,128]{1,0:T(8,128)(2,1)S(1)}, bf16[320,128]{1,0:T(8,128)(2,1)S(1)}, u32[]{:S(2)}, u32[]{:S(2)}) collective-permute-start(bf16[320,128]{1,0:T(8,128)(2,1)S(1)} %add.5), channel_id=1, source_target_pairs={{1,5},{3,7},{5,1},{7,3},{9,13},{11,15},{13,9},{15,11},{17,21},{19,... | collective-permute-start | bytes 245768 | tf_op jit(solution)/shard_map/ppermute | solution.py:41
  45.0 3.9 %collective-permute-done.15 = bf16[16,16,512]{2,1,0:T(8,128)(2,1)S(1)} collective-permute-done((bf16[16,16,512]{2,1,0:T(8,128)(2,1)S(1)}, bf16[16,16,512]{2,1,0:T(8,128)(2,1)S(1)}, u32[]{:S(2)}, u32[]{:S(2)}) %collective-permute-start.15) | collective-permute-done | bytes 262176 | tf_op jit(solution)/shard_map/ppermute | solution.py:41
  48.9 0.1 join.13
  48.9 3.1 %collective-permute-start.16 = (bf16[32,16,512]{2,1,0:T(8,128)(2,1)S(1)}, bf16[32,16,512]{2,1,0:T(8,128)(2,1)S(1)}, u32[]{:S(2)}, u32[]{:S(2)}) collective-permute-start(bf16[32,16,512]{2,1,0:T(8,128)(2,1)S(1)} %bitcast.28), channel_id=1, source_target_pairs={{0,1},{2,3},{4,5},{6,7},{8,9},{10,11},{12,13},{14,15},{16,17},{18,... | collective-permute-start | bytes 1572872 | tf_op jit(solution)/shard_map/ppermute | solution.py:47
  52.0 0.7 %collective-permute-start.10 = (bf16[640,128]{1,0:T(8,128)(2,1)S(1)}, bf16[640,128]{1,0:T(8,128)(2,1)S(1)}, u32[]{:S(2)}, u32[]{:S(2)}) collective-permute-start(bf16[640,128]{1,0:T(8,128)(2,1)S(1)} %bitcast.34), channel_id=1, source_target_pairs={{1,3},{3,1},{5,7},{7,5},{9,11},{11,9},{13,15},{15,13},{17,19},{19,... | collective-permute-start | bytes 491528 | tf_op jit(solution)/shard_map/ppermute | solution.py:41
  52.7 1.3 %collective-permute-start.11 = (bf16[1280,128]{1,0:T(8,128)(2,1)S(1)}, bf16[1280,128]{1,0:T(8,128)(2,1)S(1)}, u32[]{:S(2)}, u32[]{:S(2)}) collective-permute-start(bf16[1280,128]{1,0:T(8,128)(2,1)S(1)} %bitcast.30), channel_id=1, source_target_pairs={{1,0},{3,2},{5,4},{7,6},{9,8},{11,10},{13,12},{15,14},{17,16},{19,... | collective-permute-start | bytes 983048 | tf_op jit(solution)/shard_map/ppermute | solution.py:47
  54.0 5.8 %collective-permute-done.11.other_ref = bf16[1280,128]{1,0:T(8,128)(2,1)S(1)} collective-permute-done((bf16[1280,128]{1,0:T(8,128)(2,1)S(1)}, bf16[1280,128]{1,0:T(8,128)(2,1)S(1)}, u32[]{:S(2)}, u32[]{:S(2)}) %collective-permute-start.11) | collective-permute-done | bytes 327712 | tf_op jit(solution)/shard_map/ppermute | solution.py:47
  59.9 4.6 %grad_conv.1 = (f32[16,512]{1,0:T(8,128)}, bf16[1024,256]{1,0:T(8,128)(2,1)}) custom-call(bf16[1280,128]{1,0:T(8,128)(2,1)S(1)} %bitcast.31, bf16[1280,128]{1,0:T(8,128)(2,1)S(1)} %collective-permute-done.11.other_ref, bf16[512,512]{1,0:T(8,128)(2,1)S(1)} %bitcast.29, bf16[512,512]{1,0:T(8,128)(2,1)S(1)} %bitcast.36, ...), custom_call_target="tpu_custom_call" | custom-call | tf_op jit(solution)/shard_map/grad_conv/pallas_call | solution.py:490
  (29 shorter events, 0.4 us)
Async XLA Ops:
  0.6 1.0 %copy-start.1 = (bf16[8,128,256]{2,1,0:T(8,128)(2,1)S(1)}, bf16[8,128,256]{2,1,0:T(8,128)(2,1)}, u32[]{:S(2)}) copy-start(bf16[8,128,256]{2,1,0:T(8,128)(2,1)} %own_ref.3) | copy-start | bytes 1572868
  1.7 1.4 %copy-start.3 = (f32[16,512]{1,0:T(8,128)S(1)}, f32[16,512]{1,0:T(8,128)}, u32[]{:S(2)}) copy-start(f32[16,512]{1,0:T(8,128)} %target_ref.1) | copy-start | bytes 98308
  1.7 5.2 %copy-start = (bf16[3,3,256,512]{3,2,1,0:T(8,128)(2,1)S(1)}, bf16[3,3,256,512]{3,2,1,0:T(8,128)(2,1)}, u32[]{:S(2)}) copy-start(bf16[3,3,256,512]{3,2,1,0:T(8,128)(2,1)} %param.5) | copy-start | bytes 7077892
  1.7 5.2 %copy-start.2 = (bf16[8,128,256]{2,1,0:T(8,128)(2,1)S(1)}, bf16[8,128,256]{2,1,0:T(8,128)(2,1)}, u32[]{:S(2)}) copy-start(bf16[8,128,256]{2,1,0:T(8,128)(2,1)} %own_ref.3) | copy-start | bytes 1572868
  1.7 5.2 %copy-start.4 = (bf16[512]{0:T(512)(128)(2,1)S(1)}, bf16[512]{0:T(512)(128)(2,1)}, u32[]{:S(2)}) copy-start(bf16[512]{0:T(512)(128)(2,1)} %bias_ref.1) | copy-start | bytes 3076
  1.7 1.3 %collective-permute-start = (bf16[2,8,256]{2,1,0:T(8,128)(2,1)S(1)}, bf16[2,8,256]{2,1,0:T(8,128)(2,1)S(1)}, u32[]{:S(2)}, u32[]{:S(2)}) collective-permute-start(bf16[2,8,256]{2,1,0:T(8,128)(2,1)S(1)} %column_rims.1), channel_id=1, source_target_pairs={{0,1},{1,0},{2,3},{3,2},{4,5},{5,4},{6,7},{7,6},{8,9},{9,8},{10,11... | collective-permute-start | bytes 24584 | tf_op jit(solution)/shard_map/ppermute | solution.py:429
  3.1 6.6 %collective-permute-start.3 = (bf16[1,16,512]{2,1,0:T(8,128)(2,1)S(1)}, bf16[1,16,512]{2,1,0:T(8,128)(2,1)S(1)}, u32[]{:S(2)}, u32[]{:S(2)}) collective-permute-start(bf16[1,16,512]{2,1,0:T(8,128)(2,1)S(1)} %get-tuple-element.36), channel_id=1, source_target_pairs={{0,1},{1,0},{2,3},{3,2},{4,5},{5,4},{6,7},{7,6},{8,9},{9,8},{10,11... | collective-permute-start | bytes 49160 | tf_op jit(solution)/shard_map/ppermute | solution.py:41
  3.5 6.8 %collective-permute-start.1 = (bf16[272,256]{1,0:T(8,128)(2,1)S(1)}, bf16[272,256]{1,0:T(8,128)(2,1)S(1)}, u32[]{:S(2)}, u32[]{:S(2)}) collective-permute-start(bf16[272,256]{1,0:T(8,128)(2,1)S(1)} %get-tuple-element.29), channel_id=1, source_target_pairs={{0,2},{4,6},{8,10},{12,14},{16,18},{20,22},{24,26},{28,30},{2,0},{... | collective-permute-start | bytes 417800 | tf_op jit(solution)/shard_map/ppermute | solution.py:24
  6.2 4.2 %collective-permute-start.2 = (bf16[272,256]{1,0:T(8,128)(2,1)S(1)}, bf16[272,256]{1,0:T(8,128)(2,1)S(1)}, u32[]{:S(2)}, u32[]{:S(2)}) collective-permute-start(bf16[272,256]{1,0:T(8,128)(2,1)S(1)} %get-tuple-element.30), channel_id=1, source_target_pairs={{2,4},{6,8},{10,12},{14,16},{18,20},{22,24},{26,28},{4,2},{8,6},{1... | collective-permute-start | bytes 417800 | tf_op jit(solution)/shard_map/ppermute | solution.py:24
  12.6 3.0 %collective-permute-start.4 = (bf16[1280,128]{1,0:T(8,128)(2,1)S(1)}, bf16[1280,128]{1,0:T(8,128)(2,1)S(1)}, u32[]{:S(2)}, u32[]{:S(2)}) collective-permute-start(bf16[1280,128]{1,0:T(8,128)(2,1)S(1)} %get-tuple-element.39), channel_id=1, source_target_pairs={{0,1},{2,3},{4,5},{6,7},{8,9},{10,11},{12,13},{14,15},{16,17},{18,... | collective-permute-start | bytes 983048 | tf_op jit(solution)/shard_map/ppermute | solution.py:47
  15.7 9.8 %collective-permute-start.5 = (bf16[640,128]{1,0:T(8,128)(2,1)S(1)}, bf16[640,128]{1,0:T(8,128)(2,1)S(1)}, u32[]{:S(2)}, u32[]{:S(2)}) collective-permute-start(bf16[640,128]{1,0:T(8,128)(2,1)S(1)} %get-tuple-element.41), channel_id=1, source_target_pairs={{1,3},{3,1},{5,7},{7,5},{9,11},{11,9},{13,15},{15,13},{17,19},{19,... | collective-permute-start | bytes 491528 | tf_op jit(solution)/shard_map/ppermute | solution.py:41
  16.4 11.0 %collective-permute-start.12 = (bf16[2,16,512]{2,1,0:T(8,128)(2,1)S(1)}, bf16[2,16,512]{2,1,0:T(8,128)(2,1)S(1)}, u32[]{:S(2)}, u32[]{:S(2)}) collective-permute-start(bf16[2,16,512]{2,1,0:T(8,128)(2,1)S(1)} %bitcast.44), channel_id=1, source_target_pairs={{0,16},{2,18},{4,20},{6,22},{8,24},{10,26},{12,28},{14,30},{16,0},... | collective-permute-start | bytes 98312 | tf_op jit(solution)/shard_map/ppermute | solution.py:41
  25.6 8.0 %collective-permute-start.6 = (bf16[320,128]{1,0:T(8,128)(2,1)S(1)}, bf16[320,128]{1,0:T(8,128)(2,1)S(1)}, u32[]{:S(2)}, u32[]{:S(2)}) collective-permute-start(bf16[320,128]{1,0:T(8,128)(2,1)S(1)} %get-tuple-element.43), channel_id=1, source_target_pairs={{1,5},{3,7},{5,1},{7,3},{9,13},{11,15},{13,9},{15,11},{17,21},{19,... | collective-permute-start | bytes 245768 | tf_op jit(solution)/shard_map/ppermute | solution.py:41
  27.5 6.2 %collective-permute-start.13 = (bf16[4,16,512]{2,1,0:T(8,128)(2,1)S(1)}, bf16[4,16,512]{2,1,0:T(8,128)(2,1)S(1)}, u32[]{:S(2)}, u32[]{:S(2)}) collective-permute-start(bf16[4,16,512]{2,1,0:T(8,128)(2,1)S(1)} %bitcast.40), channel_id=1, source_target_pairs={{0,8},{2,10},{4,12},{6,14},{8,0},{10,2},{12,4},{14,6},{16,24},{18,... | collective-permute-start | bytes 196616 | tf_op jit(solution)/shard_map/ppermute | solution.py:41
  33.7 6.9 %collective-permute-start.14 = (bf16[8,16,512]{2,1,0:T(8,128)(2,1)S(1)}, bf16[8,16,512]{2,1,0:T(8,128)(2,1)S(1)}, u32[]{:S(2)}, u32[]{:S(2)}) collective-permute-start(bf16[8,16,512]{2,1,0:T(8,128)(2,1)S(1)} %bitcast.37), channel_id=1, source_target_pairs={{0,4},{2,6},{4,0},{6,2},{8,12},{10,14},{12,8},{14,10},{16,20},{18,... | collective-permute-start | bytes 393224 | tf_op jit(solution)/shard_map/ppermute | solution.py:41
  36.5 0.7 %collective-permute-start.7 = (bf16[320,128]{1,0:T(8,128)(2,1)S(1)}, bf16[320,128]{1,0:T(8,128)(2,1)S(1)}, u32[]{:S(2)}, u32[]{:S(2)}) collective-permute-start(bf16[320,128]{1,0:T(8,128)(2,1)S(1)} %add.3.keep_ref), channel_id=1, source_target_pairs={{1,9},{3,11},{5,13},{7,15},{9,1},{11,3},{13,5},{15,7},{17,25},{19,... | collective-permute-start | bytes 245768 | tf_op jit(solution)/shard_map/ppermute | solution.py:41
  40.6 8.3 %collective-permute-start.15 = (bf16[16,16,512]{2,1,0:T(8,128)(2,1)S(1)}, bf16[16,16,512]{2,1,0:T(8,128)(2,1)S(1)}, u32[]{:S(2)}, u32[]{:S(2)}) collective-permute-start(bf16[16,16,512]{2,1,0:T(8,128)(2,1)S(1)} %bitcast.32), channel_id=1, source_target_pairs={{0,2},{2,0},{4,6},{6,4},{8,10},{10,8},{12,14},{14,12},{16,18},{18,... | collective-permute-start | bytes 786440 | tf_op jit(solution)/shard_map/ppermute | solution.py:41
  43.5 0.7 %collective-permute-start.8 = (bf16[320,128]{1,0:T(8,128)(2,1)S(1)}, bf16[320,128]{1,0:T(8,128)(2,1)S(1)}, u32[]{:S(2)}, u32[]{:S(2)}) collective-permute-start(bf16[320,128]{1,0:T(8,128)(2,1)S(1)} %add.4.keep_ref), channel_id=1, source_target_pairs={{1,17},{3,19},{5,21},{7,23},{9,25},{11,27},{13,29},{15,31},{17,1},... | collective-permute-start | bytes 245768 | tf_op jit(solution)/shard_map/ppermute | solution.py:41
  44.2 0.7 %collective-permute-start.9 = (bf16[320,128]{1,0:T(8,128)(2,1)S(1)}, bf16[320,128]{1,0:T(8,128)(2,1)S(1)}, u32[]{:S(2)}, u32[]{:S(2)}) collective-permute-start(bf16[320,128]{1,0:T(8,128)(2,1)S(1)} %add.5), channel_id=1, source_target_pairs={{1,5},{3,7},{5,1},{7,3},{9,13},{11,15},{13,9},{15,11},{17,21},{19,... | collective-permute-start | bytes 245768 | tf_op jit(solution)/shard_map/ppermute | solution.py:41
  48.9 11.0 %collective-permute-start.16 = (bf16[32,16,512]{2,1,0:T(8,128)(2,1)S(1)}, bf16[32,16,512]{2,1,0:T(8,128)(2,1)S(1)}, u32[]{:S(2)}, u32[]{:S(2)}) collective-permute-start(bf16[32,16,512]{2,1,0:T(8,128)(2,1)S(1)} %bitcast.28), channel_id=1, source_target_pairs={{0,1},{2,3},{4,5},{6,7},{8,9},{10,11},{12,13},{14,15},{16,17},{18,... | collective-permute-start | bytes 1572872 | tf_op jit(solution)/shard_map/ppermute | solution.py:47
  52.0 0.7 %collective-permute-start.10 = (bf16[640,128]{1,0:T(8,128)(2,1)S(1)}, bf16[640,128]{1,0:T(8,128)(2,1)S(1)}, u32[]{:S(2)}, u32[]{:S(2)}) collective-permute-start(bf16[640,128]{1,0:T(8,128)(2,1)S(1)} %bitcast.34), channel_id=1, source_target_pairs={{1,3},{3,1},{5,7},{7,5},{9,11},{11,9},{13,15},{15,13},{17,19},{19,... | collective-permute-start | bytes 491528 | tf_op jit(solution)/shard_map/ppermute | solution.py:41
  52.7 7.1 %collective-permute-start.11 = (bf16[1280,128]{1,0:T(8,128)(2,1)S(1)}, bf16[1280,128]{1,0:T(8,128)(2,1)S(1)}, u32[]{:S(2)}, u32[]{:S(2)}) collective-permute-start(bf16[1280,128]{1,0:T(8,128)(2,1)S(1)} %bitcast.30), channel_id=1, source_target_pairs={{1,0},{3,2},{5,4},{7,6},{9,8},{11,10},{13,12},{15,14},{17,16},{19,... | collective-permute-start | bytes 983048 | tf_op jit(solution)/shard_map/ppermute | solution.py:47
